TPU v7x, 512 devices: a whole 4x8x8 slice. The times are simulated.
512 devices in a mesh: seq: 16 (over x_hi, y), chan: 32 (over z, x_lo, core).
Axes of the slice: x: 4 (x_hi: 2, x_lo: 2; x = x_hi * 2 + x_lo), y: 8, z: 8, core: 2. Of those that a mesh axis runs over, the one named last changes fastest.
Arguments:
- query_gate: bfloat16 [8192, 8192], P('seq', 'chan'), may hold values from -6 to 6
- key_gate: bfloat16 [8192, 8192], P('seq', 'chan'), may hold values from -6 to 6
- values_in: bfloat16 [8192, 8192], P('seq', 'chan'), may hold values from -6 to 6
- cotangent: bfloat16 [8192, 8192], P('seq', 'chan'), may hold values from -6 to 6
- decay_rate: float32 [512, 16], P('chan'), may hold values from 3.6621094e-05 to 0.0333333333, as said below
- residues: float32 [512, 16], P('chan'), may hold values from -1.5 to 1.5
Outputs:
- mixed_out: bfloat16 [8192, 8192], P('seq', 'chan')
- query_grad: bfloat16 [8192, 8192], P('seq', 'chan')
- key_grad: bfloat16 [8192, 8192], P('seq', 'chan')
- value_grad: bfloat16 [8192, 8192], P('seq', 'chan')
- residue_grad: float32 [512, 16], P('chan')
Inputs may be any that keep to these rules, and one draw needn't show every extreme that they name: `decay_rate`: positive decay rates.
All inputs are finite; a program needn't handle non-finite values.
Results may differ from a plain program's by a relative error of at most 0.005.
Values may be sent and summed in bfloat16 or wider, within the bound.
A program may use at most 64 MiB of HBM per device.

v0:
```python
import jax
import jax.numpy as jnp
from jax import lax
from jax.sharding import PartitionSpec as P

GROUP = 16


block_rows = 64
precise = lax.Precision.HIGHEST


def local_part(signal, decay_rate, scaled):
    length, channels = signal.shape
    groups, mode_count = decay_rate.shape
    blocks = length // block_rows
    pieces = signal.reshape(blocks, block_rows, groups, GROUP)
    offsets = jnp.arange(block_rows, dtype=jnp.float32)
    distance = offsets[:, None] - offsets[None, :]
    causal = distance >= 0
    powers = jnp.where(
        causal, jnp.exp(-decay_rate[:, :, None, None] * jnp.maximum(distance, 0.0)), 0.0
    )
    kernel = jnp.einsum("gm,gmts->gts", scaled, powers, precision=precise)
    inner_part = jnp.einsum("gts,jsgc->jtgc", kernel, pieces, precision=precise)
    tail_power = jnp.exp(-decay_rate[:, :, None] * (block_rows - 1.0 - offsets))
    block_ends = jnp.einsum("gms,jsgc->jgmc", tail_power, pieces, precision=precise)
    row_index = jnp.arange(blocks + 1, dtype=jnp.float32)
    col_index = jnp.arange(blocks, dtype=jnp.float32)
    block_gap = row_index[:, None] - 1.0 - col_index[None, :]
    spread = jnp.where(
        block_gap >= 0,
        jnp.exp(-decay_rate[:, :, None, None] * block_rows * jnp.maximum(block_gap, 0.0)),
        0.0,
    )
    starts = jnp.einsum("gmji,igmc->jgmc", spread, block_ends, precision=precise)
    local_end = jnp.transpose(starts[blocks], (1, 0, 2)).reshape(mode_count, channels)
    return (pieces, powers, inner_part, starts[:blocks], local_end)


def finish(parts, decay_rate, scaled, entry):
    pieces, powers, inner_part, starts, local_end = parts
    blocks = starts.shape[0]
    groups, mode_count = decay_rate.shape
    entry_state = jnp.transpose(entry.reshape(mode_count, groups, GROUP), (1, 0, 2))
    block_index = jnp.arange(blocks, dtype=jnp.float32)
    lift_power = jnp.exp(-decay_rate[None, :, :] * block_rows * block_index[:, None, None])
    full_starts = starts + lift_power[..., None] * entry_state[None]
    offsets = jnp.arange(block_rows, dtype=jnp.float32)
    head_power = scaled[:, :, None] * jnp.exp(-decay_rate[:, :, None] * (offsets + 1.0))
    outer_part = jnp.einsum("gmt,jgmc->jtgc", head_power, full_starts, precision=precise)
    result = (inner_part + outer_part).reshape(blocks * block_rows, groups * GROUP)
    return (result, full_starts)


def residue_sums(pieces, powers, full_starts, slope_grad, decay_rate):
    grads = slope_grad.reshape(pieces.shape)
    offsets = jnp.arange(block_rows, dtype=jnp.float32)
    pair_sums = jnp.einsum("jtgc,jsgc->jgts", grads, pieces, precision=precise)
    within = jnp.einsum("jgts,gmts->gm", pair_sums, powers, precision=precise)
    rise_power = jnp.exp(-decay_rate[:, :, None] * (offsets + 1.0))
    across = jnp.einsum("gmt,jtgc,jgmc->gm", rise_power, grads, full_starts, precision=precise)
    return (within + across) * jnp.sqrt(1.0 - jnp.exp(-2.0 * decay_rate))


def hyena_local(query_gate, key_gate, values_in, cotangent, decay_rate, scaled, carry_fn):
    query_f = query_gate.astype(jnp.float32)
    cot_f = cotangent.astype(jnp.float32)
    gated_low = (key_gate.astype(jnp.float32) * values_in.astype(jnp.float32)).astype(jnp.bfloat16)
    gated_in = lax.optimization_barrier(gated_low).astype(jnp.float32)
    slope_grad = cot_f * query_f
    forward = local_part(gated_in, decay_rate, scaled)
    backward = local_part(slope_grad[::-1], decay_rate, scaled)
    forward_entry, backward_entry = carry_fn(forward[4], backward[4])
    convolved, full_starts = finish(forward, decay_rate, scaled, forward_entry)
    reversed_out, unused_starts = finish(backward, decay_rate, scaled, backward_entry)
    gated_grad = reversed_out[::-1]
    terms = residue_sums(forward[0], forward[1], full_starts, slope_grad, decay_rate)
    mixed_out = (query_f * convolved).astype(jnp.bfloat16)
    query_grad = (cot_f * convolved).astype(jnp.bfloat16)
    key_grad = (gated_grad * values_in.astype(jnp.float32)).astype(jnp.bfloat16)
    value_grad = (gated_grad * key_gate.astype(jnp.float32)).astype(jnp.bfloat16)
    return (mixed_out, query_grad, key_grad, value_grad, terms)


def no_carry(forward_last, backward_last):
    return (jnp.zeros_like(forward_last), jnp.zeros_like(backward_last))


def body(query_gate, key_gate, values_in, cotangent, decay_rate, residues):
    scaled = residues * jnp.sqrt(1.0 - jnp.exp(-2.0 * decay_rate))
    moved = (
        lax.all_to_all(query_gate, "seq", split_axis=1, concat_axis=0, tiled=True),
        lax.all_to_all(key_gate, "seq", split_axis=1, concat_axis=0, tiled=True),
        lax.all_to_all(values_in, "seq", split_axis=1, concat_axis=0, tiled=True),
        lax.all_to_all(cotangent, "seq", split_axis=1, concat_axis=0, tiled=True),
    )
    query_here, key_here, value_here, cot_here = moved
    groups = query_here.shape[1] // GROUP
    first_group = lax.axis_index("seq") * groups
    rate_here = lax.dynamic_slice_in_dim(decay_rate, first_group, groups, 0)
    scaled_here = lax.dynamic_slice_in_dim(scaled, first_group, groups, 0)
    mixed_out, query_grad, key_grad, value_grad, terms = hyena_local(
        query_here, key_here, value_here, cot_here, rate_here, scaled_here, no_carry
    )
    returned = (
        lax.all_to_all(mixed_out, "seq", split_axis=0, concat_axis=1, tiled=True),
        lax.all_to_all(query_grad, "seq", split_axis=0, concat_axis=1, tiled=True),
        lax.all_to_all(key_grad, "seq", split_axis=0, concat_axis=1, tiled=True),
        lax.all_to_all(value_grad, "seq", split_axis=0, concat_axis=1, tiled=True),
    )
    residue_grad = lax.all_gather(terms, "seq", axis=0, tiled=True)
    return (returned[0], returned[1], returned[2], returned[3], residue_grad)


def solution(mesh):
    return jax.shard_map(
        body,
        mesh=mesh,
        in_specs=(
            P("seq", "chan"),
            P("seq", "chan"),
            P("seq", "chan"),
            P("seq", "chan"),
            P("chan", None),
            P("chan", None),
        ),
        out_specs=(
            P("seq", "chan"),
            P("seq", "chan"),
            P("seq", "chan"),
            P("seq", "chan"),
            P("chan", None),
        ),
        check_vma=False,
    )
```

profile of v0, /device:TPU:128, one launch (start us, length us, event | category | flops | bytes accessed | tf_op | source)
XLA Modules:
  0.0 179.2 jit_solution(13311337386671779280)
XLA Ops:
  0.7 1.9 %copy.41 = bf16[512,256]{0,1:T(8,128)(2,1)} copy(bf16[512,256]{1,0:T(8,128)(2,1)} %param.6) | data formatting | bytes 524288 | tf_op args[0]
  2.5 9.8 %all-to-all-start = ((bf16[512,16,16]{0,2,1:T(8,128)(2,1)}), bf16[512,16,16]{0,2,1:T(8,128)(2,1)S(1)}, u32[]{:S(2)}, u32[]{:S(2)}) async-start(bf16[512,16,16]{0,2,1:T(8,128)(2,1)} %bitcast.2), calls=%async_computation | async-start | bytes 524288 | tf_op jit(solution)/shard_map/all_to_all | solution.py:93
  12.3 0.5 iota_subtract_fusion.2
  12.9 0.7 broadcast_multiply_fusion
  14.1 0.8 copy.52
  15.2 8.7 %all-to-all-done = bf16[512,16,16]{0,2,1:T(8,128)(2,1)S(1)} async-done(((bf16[512,16,16]{0,2,1:T(8,128)(2,1)}), bf16[512,16,16]{0,2,1:T(8,128)(2,1)S(1)}, u32[]{:S(2)}, u32[]{:S(2)}) %all-to-all-start) | async-done | bytes 262176 | tf_op jit(solution)/shard_map/all_to_all | solution.py:93
  23.9 4.5 %all-to-all-start.4 = ((bf16[512,16,16]{0,2,1:T(8,128)(2,1)}), bf16[512,16,16]{0,2,1:T(8,128)(2,1)S(1)}, u32[]{:S(2)}, u32[]{:S(2)}) async-start(bf16[512,16,16]{0,2,1:T(8,128)(2,1)} %bitcast.28), calls=%async_computation.4 | async-start | bytes 524288 | tf_op jit(solution)/shard_map/all_to_all | solution.py:96
  28.4 1.3 fusion.49
  29.8 0.8 copy.42
  30.6 0.8 copy.44
  31.6 1.4 fusion.16
  33.0 6.5 %all-to-all-done.4 = bf16[512,16,16]{0,2,1:T(8,128)(2,1)S(1)} async-done(((bf16[512,16,16]{0,2,1:T(8,128)(2,1)}), bf16[512,16,16]{0,2,1:T(8,128)(2,1)S(1)}, u32[]{:S(2)}, u32[]{:S(2)}) %all-to-all-start.4) | async-done | bytes 262176 | tf_op jit(solution)/shard_map/all_to_all | solution.py:96
  39.5 4.5 %all-to-all-start.1 = ((bf16[512,16,16]{0,2,1:T(8,128)(2,1)}), bf16[512,16,16]{0,2,1:T(8,128)(2,1)S(1)}, u32[]{:S(2)}, u32[]{:S(2)}) async-start(bf16[512,16,16]{0,2,1:T(8,128)(2,1)} %bitcast.4), calls=%async_computation.1 | async-start | bytes 524288 | tf_op jit(solution)/shard_map/all_to_all | solution.py:94
  44.3 4.6 %rev.6 = f32[8192,16]{0,1:T(8,128)S(1)} reverse(f32[8192,16]{0,1:T(8,128)S(1)} %bitcast.149), dimensions={0} | reverse | bytes 1048576 | tf_op jit(solution)/shard_map/rev | solution.py:73
  48.8 0.5 reshape.474
  49.5 1.0 convolution_bitcast_fusion.2
  50.6 1.9 %convolution_bitcast_fusion = f32[129,1,16,16]{0,3,2,1:T(8,128)S(1)} fusion(f32[129,128]{1,0:T(8,128)S(1)} %fusion.27, f32[16]{0:T(128)S(1)} %copy-done.24, pred[129,128]{1,0:T(8,128)(4,1)S(1)} %fusion.28, f32[128,16,16]{0,1,2:T(8,128)S(1)} %convolution_bitcast_fusion.2), kind=kOutput, calls=%fused_computation.4 | convolution fusion | flops 51253248 | bytes 345792 | tf_op jit(solution)/shard_map/gmji,igmc->jgmc/dot_general | solution.py:36
  52.6 1.3 fusion.51
  53.9 1.3 all-to-all-done.1
  55.1 8.4 %all-to-all-start.2 = ((bf16[512,16,16]{0,2,1:T(8,128)(2,1)}), bf16[512,16,16]{0,2,1:T(8,128)(2,1)}, u32[]{:S(2)}, u32[]{:S(2)}) async-start(bf16[512,16,16]{0,2,1:T(8,128)(2,1)} %bitcast.6), calls=%async_computation.2 | async-start | bytes 524288 | tf_op jit(solution)/shard_map/all_to_all | solution.py:95
  63.6 0.7 fusion
  65.0 4.6 %rev.7 = f32[8192,16]{0,1:T(8,128)S(1)} reverse(f32[8192,16]{0,1:T(8,128)S(1)} %reshape.477), dimensions={0} | reverse | bytes 1048576 | tf_op jit(solution)/shard_map/rev | solution.py:77
  69.8 4.4 %all-to-all-done.2 = bf16[512,16,16]{0,2,1:T(8,128)(2,1)} async-done(((bf16[512,16,16]{0,2,1:T(8,128)(2,1)}), bf16[512,16,16]{0,2,1:T(8,128)(2,1)}, u32[]{:S(2)}, u32[]{:S(2)}) %all-to-all-start.2) | async-done | bytes 262176 | tf_op jit(solution)/shard_map/all_to_all | solution.py:95
  74.1 1.0 convert_bitcast_fusion.2
  75.2 0.8 multiply_convert_fusion
  76.0 0.5 reshape.469
  76.6 0.6 convolution_bitcast_fusion.3
  77.2 0.7 fusion.50
  77.9 1.9 %convolution_bitcast_fusion.1 = f32[129,1,16,16]{0,3,2,1:T(8,128)S(1)} fusion(f32[129,128]{1,0:T(8,128)S(1)} %copy-done.9, f32[16]{0:T(128)S(1)} %copy-done.25, pred[129,128]{1,0:T(8,128)(4,1)S(1)} %copy-done.15, f32[128,16,16]{0,1,2:T(8,128)S(1)} %convolution_bitcast_fusion.3), kind=kOutput, calls=%fused_computation.5 | convolution fusion | flops 51253248 | bytes 345792 | tf_op jit(solution)/shard_map/gmji,igmc->jgmc/dot_general | solution.py:36
  79.9 0.7 fusion.1
  81.2 1.0 fusion.15
  82.2 15.6 %all_to_all.122 = bf16[16,512,16]{1,2,0:T(8,128)(2,1)S(1)} all-to-all(bf16[16,512,16]{1,2,0:T(8,128)(2,1)S(1)} %get-tuple-element.23), channel_id=1, replica_groups=mesh['seq'=16,'chan'=32] {'seq'}, dimensions={0} | all-to-all | bytes 524288 | tf_op jit(solution)/shard_map/all_to_all | solution.py:107
  97.9 4.1 %all-to-all-start.5 = ((bf16[16,512,16]{1,2,0:T(8,128)(2,1)}), bf16[16,512,16]{1,2,0:T(8,128)(2,1)S(1)}, u32[]{:S(2)}, u32[]{:S(2)}) async-start(bf16[16,512,16]{1,2,0:T(8,128)(2,1)} %get-tuple-element.22), calls=%async_computation.5 | async-start | bytes 524288 | tf_op jit(solution)/shard_map/all_to_all | solution.py:108
  102.0 0.7 copy.112
  102.7 9.7 %all-to-all-done.5 = bf16[16,512,16]{1,2,0:T(8,128)(2,1)S(1)} async-done(((bf16[16,512,16]{1,2,0:T(8,128)(2,1)}), bf16[16,512,16]{1,2,0:T(8,128)(2,1)S(1)}, u32[]{:S(2)}, u32[]{:S(2)}) %all-to-all-start.5) | async-done | bytes 262176 | tf_op jit(solution)/shard_map/all_to_all | solution.py:108
  112.5 4.3 %all-to-all-start.6 = ((bf16[16,512,16]{1,2,0:T(8,128)(2,1)}), bf16[16,512,16]{1,2,0:T(8,128)(2,1)}, u32[]{:S(2)}, u32[]{:S(2)}) async-start(bf16[16,512,16]{1,2,0:T(8,128)(2,1)} %bitcast.148), calls=%async_computation.6 | async-start | bytes 524288 | tf_op jit(solution)/shard_map/all_to_all | solution.py:109
  117.3 0.7 copy.111
  118.1 1.0 convolution_bitcast_fusion.4
  119.1 8.2 %all-to-all-done.6 = bf16[16,512,16]{1,2,0:T(8,128)(2,1)} async-done(((bf16[16,512,16]{1,2,0:T(8,128)(2,1)}), bf16[16,512,16]{1,2,0:T(8,128)(2,1)}, u32[]{:S(2)}, u32[]{:S(2)}) %all-to-all-start.6) | async-done | bytes 262176 | tf_op jit(solution)/shard_map/all_to_all | solution.py:109
  127.3 4.3 %all-to-all-start.7 = ((bf16[16,512,16]{1,2,0:T(8,128)(2,1)}), bf16[16,512,16]{1,2,0:T(8,128)(2,1)S(1)}, u32[]{:S(2)}, u32[]{:S(2)}) async-start(bf16[16,512,16]{1,2,0:T(8,128)(2,1)} %bitcast.147), calls=%async_computation.7 | async-start | bytes 524288 | tf_op jit(solution)/shard_map/all_to_all | solution.py:110
  131.9 0.8 fusion.3
  132.7 0.7 fusion.46
  133.4 40.9 %all-gather = f32[16,1,16]{2,1,0:T(1,128)S(1)} all-gather(f32[1,1,16]{2,1,0:T(1,128)S(1)} %fusion.46), channel_id=1, replica_groups=mesh['seq'=16,'chan'=32] {'seq'}, dimensions={0}, use_global_device_ids=true | all-gather | bytes 1088 | tf_op jit(solution)/shard_map/all_gather | solution.py:112
  174.3 0.8 copy.67
  175.1 0.8 copy.68
  175.9 1.8 copy.69
  177.7 0.8 copy.70
  178.6 0.6 copy.114
  (75 shorter events, 3.7 us)
Async XLA Ops:
  0.6 13.5 %copy-start.3 = (bf16[512,256]{1,0:T(8,128)(2,1)S(1)}, bf16[512,256]{1,0:T(8,128)(2,1)}, u32[]{:S(2)}) copy-start(bf16[512,256]{1,0:T(8,128)(2,1)} %param.9) | copy-start | bytes 786436
  0.6 29.1 %copy-start.4 = (bf16[512,256]{1,0:T(8,128)(2,1)S(1)}, bf16[512,256]{1,0:T(8,128)(2,1)}, u32[]{:S(2)}) copy-start(bf16[512,256]{1,0:T(8,128)(2,1)} %param.7) | copy-start | bytes 786436
  2.5 28.1 %copy-start.5 = (bf16[512,256]{1,0:T(8,128)(2,1)S(1)}, bf16[512,256]{1,0:T(8,128)(2,1)}, u32[]{:S(2)}) copy-start(bf16[512,256]{1,0:T(8,128)(2,1)} %param.8) | copy-start | bytes 786436
  2.5 21.4 %all-to-all-start = ((bf16[512,16,16]{0,2,1:T(8,128)(2,1)}), bf16[512,16,16]{0,2,1:T(8,128)(2,1)S(1)}, u32[]{:S(2)}, u32[]{:S(2)}) async-start(bf16[512,16,16]{0,2,1:T(8,128)(2,1)} %bitcast.2), calls=%async_computation | async-start | bytes 524288 | tf_op jit(solution)/shard_map/all_to_all | solution.py:93
  12.9 18.6 %copy-start.6 = (f32[64,64]{1,0:T(8,128)}, f32[64,64]{1,0:T(8,128)S(1)}, u32[]{:S(2)}) copy-start(f32[64,64]{1,0:T(8,128)S(1)} %fusion.29) | copy-start | bytes 49156
  13.6 0.5 copy-start.23
  13.6 50.0 %copy-start.10 = (f32[16]{0:T(128)}, f32[16]{0:T(128)S(1)}, u32[]{:S(2)}) copy-start(f32[16]{0:T(128)S(1)} %get-tuple-element.16) | copy-start | bytes 196
  14.1 49.5 %copy-start.16 = (f32[64]{0:T(128)}, f32[64]{0:T(128)S(1)}, u32[]{:S(2)}) copy-start(f32[64]{0:T(128)S(1)} %iota_add_fusion.1) | copy-start | bytes 772
  15.1 35.5 %copy-start.14 = (pred[129,128]{1,0:T(8,128)(4,1)}, pred[129,128]{1,0:T(8,128)(4,1)S(1)}, u32[]{:S(2)}) copy-start(pred[129,128]{1,0:T(8,128)(4,1)S(1)} %fusion.28) | copy-start | bytes 49540
  15.2 35.4 %copy-start.8 = (f32[129,128]{1,0:T(8,128)}, f32[129,128]{1,0:T(8,128)S(1)}, u32[]{:S(2)}) copy-start(f32[129,128]{1,0:T(8,128)S(1)} %fusion.27) | copy-start | bytes 198148
  23.9 15.6 %all-to-all-start.4 = ((bf16[512,16,16]{0,2,1:T(8,128)(2,1)}), bf16[512,16,16]{0,2,1:T(8,128)(2,1)S(1)}, u32[]{:S(2)}, u32[]{:S(2)}) async-start(bf16[512,16,16]{0,2,1:T(8,128)(2,1)} %bitcast.28), calls=%async_computation.4 | async-start | bytes 524288 | tf_op jit(solution)/shard_map/all_to_all | solution.py:96
  33.0 19.6 %copy-start.1 = (f32[1,64,64]{2,0,1:T(1,128)}, f32[1,64,64]{2,0,1:T(1,128)S(1)}, u32[]{:S(2)}) copy-start(f32[1,64,64]{2,0,1:T(1,128)S(1)} %fusion.16) | copy-start | bytes 49156
  39.5 15.6 %all-to-all-start.1 = ((bf16[512,16,16]{0,2,1:T(8,128)(2,1)}), bf16[512,16,16]{0,2,1:T(8,128)(2,1)S(1)}, u32[]{:S(2)}, u32[]{:S(2)}) async-start(bf16[512,16,16]{0,2,1:T(8,128)(2,1)} %bitcast.4), calls=%async_computation.1 | async-start | bytes 524288 | tf_op jit(solution)/shard_map/all_to_all | solution.py:94
  48.8 0.7 copy-start.21
  48.8 1.8 copy-start.24
  52.5 11.1 %copy-start.19 = (f32[16]{0:T(128)S(1)}, f32[16]{0:T(128)}, u32[]{:S(2)}) copy-start(f32[16]{0:T(128)} %fusion.49) | copy-start | bytes 196
  55.1 19.0 %all-to-all-start.2 = ((bf16[512,16,16]{0,2,1:T(8,128)(2,1)}), bf16[512,16,16]{0,2,1:T(8,128)(2,1)}, u32[]{:S(2)}, u32[]{:S(2)}) async-start(bf16[512,16,16]{0,2,1:T(8,128)(2,1)} %bitcast.6), calls=%async_computation.2 | async-start | bytes 524288 | tf_op jit(solution)/shard_map/all_to_all | solution.py:95
  75.2 1.4 copy-start.11
  75.2 1.4 copy-start.22
  76.0 1.2 copy-start.2
  76.5 1.3 copy-start.9
  76.6 1.3 copy-start.15
  76.6 1.3 copy-start.25
  77.1 2.7 %copy-start.12 = (f32[16]{0:T(128)S(1)}, f32[16]{0:T(128)}, u32[]{:S(2)}) copy-start(f32[16]{0:T(128)} %copy-done.10) | copy-start | bytes 196
  77.2 2.7 %copy-start.17 = (f32[64]{0:T(128)S(1)}, f32[64]{0:T(128)}, u32[]{:S(2)}) copy-start(f32[64]{0:T(128)} %copy-done.16) | copy-start | bytes 772
  77.2 2.7 %copy-start.20 = (f32[16]{0:T(128)S(1)}, f32[16]{0:T(128)}, u32[]{:S(2)}) copy-start(f32[16]{0:T(128)} %fusion.49) | copy-start | bytes 196
  81.2 20.8 %copy-start = (bf16[8192,16]{0,1:T(8,128)(2,1)S(1)}, bf16[8192,16]{0,1:T(8,128)(2,1)}, u32[]{:S(2)}) copy-start(bf16[8192,16]{0,1:T(8,128)(2,1)} %get-tuple-element.21) | copy-start | bytes 786436
  97.9 14.6 %all-to-all-start.5 = ((bf16[16,512,16]{1,2,0:T(8,128)(2,1)}), bf16[16,512,16]{1,2,0:T(8,128)(2,1)S(1)}, u32[]{:S(2)}, u32[]{:S(2)}) async-start(bf16[16,512,16]{1,2,0:T(8,128)(2,1)} %get-tuple-element.22), calls=%async_computation.5 | async-start | bytes 524288 | tf_op jit(solution)/shard_map/all_to_all | solution.py:108
  112.5 14.8 %all-to-all-start.6 = ((bf16[16,512,16]{1,2,0:T(8,128)(2,1)}), bf16[16,512,16]{1,2,0:T(8,128)(2,1)}, u32[]{:S(2)}, u32[]{:S(2)}) async-start(bf16[16,512,16]{1,2,0:T(8,128)(2,1)} %bitcast.148), calls=%async_computation.6 | async-start | bytes 524288 | tf_op jit(solution)/shard_map/all_to_all | solution.py:109
  118.0 13.5 %copy-start.7 = (f32[64,64]{1,0:T(8,128)S(1)}, f32[64,64]{1,0:T(8,128)}, u32[]{:S(2)}) copy-start(f32[64,64]{1,0:T(8,128)} %copy-done.6) | copy-start | bytes 49156
  118.0 13.6 %copy-start.13 = (f32[16]{0:T(128)S(1)}, f32[16]{0:T(128)}, u32[]{:S(2)}) copy-start(f32[16]{0:T(128)} %copy-done.10) | copy-start | bytes 196
  118.0 13.9 %copy-start.18 = (f32[64]{0:T(128)S(1)}, f32[64]{0:T(128)}, u32[]{:S(2)}) copy-start(f32[64]{0:T(128)} %copy-done.16) | copy-start | bytes 772
  127.3 50.5 %all-to-all-start.7 = ((bf16[16,512,16]{1,2,0:T(8,128)(2,1)}), bf16[16,512,16]{1,2,0:T(8,128)(2,1)S(1)}, u32[]{:S(2)}, u32[]{:S(2)}) async-start(bf16[16,512,16]{1,2,0:T(8,128)(2,1)} %bitcast.147), calls=%async_computation.7 | async-start | bytes 524288 | tf_op jit(solution)/shard_map/all_to_all | solution.py:110
where the time goes:
time: 180 us; the launch traced here: 179 us
  blocking collectives  56.5 us (31%)
  starting transfers between devices  40 us (22%)
  waiting for transfers between devices  38.9 us (22%)
  local copies, waits for them, and re-layouts  23.6 us (13%)
  matrix products  12 us (7%)
  other arithmetic  7.13 us (4%)
    all_gather x1, blocking collectives, body(): residue_grad = lax.all_gather(terms, 'seq', axis=0, tiled=True)  40.9 us
    all_to_all x1, blocking collectives, body(): lax.all_to_all(mixed_out, 'seq', split_axis=0, concat_axis=1, tiled=True)  15.6 us
    unnamed x61, local copies, waits for them, and re-layouts  10 us
    all_to_all x1, starting transfers between devices, body(): lax.all_to_all(query_gate, 'seq', split_axis=1, concat_axis=0, tiled=True)  9.8 us
    all_to_all x1, waiting for transfers between devices, body(): lax.all_to_all(query_grad, 'seq', split_axis=0, concat_axis=1, tiled=True)  9.73 us
    all_to_all x1, waiting for transfers between devices, body(): lax.all_to_all(query_gate, 'seq', split_axis=1, concat_axis=0, tiled=True)  8.74 us
    all_to_all x1, starting transfers between devices, body(): lax.all_to_all(values_in, 'seq', split_axis=1, concat_axis=0, tiled=True)  8.41 us
    all_to_all x1, waiting for transfers between devices, body(): lax.all_to_all(key_grad, 'seq', split_axis=0, concat_axis=1, tiled=True)  8.2 us
  transfers between devices with their start and end apart: 7, of which 6 were waited for; matrix products, arithmetic and copies ran while one was open for 17% of the time, Pallas kernels for 0%

commit v1 on v0

v1 whole, which is shorter than its diff:
```python
import jax
import jax.numpy as jnp
from jax import lax
from jax.experimental import pallas as pl
from jax.experimental.pallas import tpu as pltpu
from jax.sharding import PartitionSpec as P

MESH = pl.DeviceIdType.MESH
f32 = jnp.float32
bf16 = jnp.bfloat16
GROUP = 16
MODES = 16
L = 64
QUARTER = 64
HIGH = lax.Precision.HIGHEST


def dot(a, b, dims=((1,), (0,)), precision=None):
    return lax.dot_general(
        a, b, (dims, ((), ())), precision=precision, preferred_element_type=f32
    )


def split(x):
    hi = x.astype(bf16)
    return hi, (x - hi.astype(f32)).astype(bf16)


def iota(shape, axis):
    return lax.broadcasted_iota(jnp.int32, shape, axis)


def pick_rows(m, rows):
    left = iota((rows, 128), 1) < QUARTER
    return jnp.concatenate(
        [
            jnp.where(left, m[:rows, :128], m[rows : 2 * rows, :128]),
            jnp.where(left, m[2 * rows : 3 * rows, 128:], m[3 * rows :, 128:]),
        ],
        axis=1,
    )


def kernel(
    peers,
    q_hbm, k_hbm, v_hbm, c_hbm, rate_hbm, res_hbm,
    mixed_ref, qgrad_ref, kgrad_ref, vgrad_ref, rgrad_ref,
    rate_ref, res_ref, q_s, k_s, v_s, c_s, x_s, sh_s, sl_s, conv_s, grad_s, fwd_s, bwd_s, bend_s,
    box, wbox, in_sem, send_sem, recv_sem,
):
    length = q_s.shape[0]
    width = q_s.shape[1]
    chunks = length // L
    me = lax.axis_index("seq")
    n = lax.axis_size("seq")
    loads = [
        pltpu.make_async_copy(src, dst, in_sem.at[i])
        for i, (src, dst) in enumerate(
            (
                (rate_hbm, rate_ref), (res_hbm, res_ref),
                (k_hbm, k_s), (v_hbm, v_s), (c_hbm, c_s), (q_hbm, q_s),
            )
        )
    ]
    for copy in loads:
        copy.start()
    ids = [peers(me, i) for i in range(n - 1)]
    barrier = pltpu.get_barrier_semaphore()
    for peer in ids:
        pl.semaphore_signal(barrier, inc=1, device_id={"seq": peer}, device_id_type=MESH)

    loads[0].wait()
    loads[1].wait()
    rate = rate_ref[...]
    factor = jnp.sqrt(1.0 - jnp.exp(-2.0 * rate))
    scaled = res_ref[...] * factor
    lane_hi = iota((16, width), 1) // GROUP
    lane_lo = iota((16, width), 1) % GROUP
    row16 = iota((16, width), 0)
    in_group = (lane_hi == row16).astype(f32)
    in_mode = (lane_lo == row16).astype(f32)
    rate_mc = dot(rate, in_group, ((0,), (0,)), HIGH)

    def row_of(x):
        return jnp.sum(dot(x, in_mode, precision=HIGH) * in_group, axis=0, keepdims=True)

    rate_row, scaled_row, factor_row = row_of(rate), row_of(scaled), row_of(factor)

    lane = iota((16, width), 1)
    position = (lane % L).astype(f32)
    end_parts = []
    start_parts = []
    for quarter in range(4):
        spread = (row16 == quarter * 4 + lane // L).astype(f32)
        rates = dot(rate, spread, ((0,), (0,)), HIGH)
        end_parts.append(jnp.exp((position - (L - 1.0)) * rates))
        start_parts.append(jnp.exp(-position * rates))
    end_hi, end_lo = zip(*[split(x) for x in end_parts])
    start_hi, start_lo = zip(*[split(x) for x in start_parts])

    def halves(hi, lo):
        return [
            jnp.concatenate([hi[2 * h], hi[2 * h + 1], lo[2 * h], lo[2 * h + 1]], axis=0)
            for h in range(2)
        ]

    end_pow = halves(end_hi, end_lo)
    start_pow = halves(start_hi, start_lo)

    lane64 = iota((L, width), 1)
    mask_i = [((lane64 // GROUP) % 4 == i).astype(bf16) for i in range(4)]
    mask_q = [(lane64 // QUARTER == q).astype(bf16) for q in range(4)]

    def spread_i(x):
        return jnp.concatenate([x * m for m in mask_i], axis=0)

    left16 = iota((16, 128), 1) < QUARTER

    def state_of(tables, pieces):
        out = []
        for h in range(2):
            first, *rest = pieces
            r = dot(tables[h], first[:, 128 * h : 128 * h + 128])
            r = r[:32] + r[32:]
            for piece in rest:
                r = r + dot(tables[h][:32], piece[:, 128 * h : 128 * h + 128])
            out.append(jnp.where(left16, r[:16], r[16:]))
        return jnp.concatenate(out, axis=1)

    decay_chunk = jnp.exp(-float(L) * rate_mc)
    decay_len = jnp.exp(-float(length) * rate_mc)
    decay_one = jnp.exp(-rate_mc)

    loads[2].wait()
    loads[3].wait()
    state = jnp.zeros((16, width), f32)
    for j in range(chunks):
        rows = pl.ds(j * L, L)
        x = (k_s[rows, :].astype(f32) * v_s[rows, :].astype(f32)).astype(bf16)
        x_s[rows, :] = x
        fwd_s[j] = state
        state = state * decay_chunk + state_of(end_pow, [spread_i(x)])
    end_state = state.astype(bf16)

    loads[4].wait()
    loads[5].wait()
    state = jnp.zeros((16, width), f32)
    for j in reversed(range(chunks)):
        rows = pl.ds(j * L, L)
        hi, lo = split(c_s[rows, :].astype(f32) * q_s[rows, :].astype(f32))
        sh_s[rows, :] = hi
        sl_s[rows, :] = lo
        bwd_s[j] = state
        here = state_of(start_pow, [spread_i(hi), spread_i(lo)])
        bend_s[j] = here
        state = state * decay_chunk + here
    box[0, me] = state.astype(bf16)
    box[1, me] = end_state

    pl.semaphore_wait(barrier, n - 1)
    sends = []
    for batch in range(2):
        for peer in ids:
            later = (peer > me).astype(jnp.int32)
            half = later if batch == 0 else 1 - later
            copy = pltpu.make_async_remote_copy(
                src_ref=box.at[half, me],
                dst_ref=box.at[batch, me],
                send_sem=send_sem.at[batch, peer],
                recv_sem=recv_sem.at[batch, me],
                device_id={"seq": peer},
                device_id_type=MESH,
            )
            copy.start()
            sends.append(copy)

    step = iota((L, width), 0).astype(f32)
    fall = jnp.exp(-step * rate_row)
    rise = jnp.exp(step * rate_row)
    q_of = iota((L, width), 1) // QUARTER
    fall_q = [jnp.where(q_of == q, fall, 0.0) for q in range(4)]
    rise_q = [jnp.where(q_of == q, rise, 0.0) for q in range(4)]
    fall_rows = jnp.concatenate(fall_q, axis=0)
    rise_rows = jnp.concatenate(rise_q, axis=0)

    def column(x):
        wide = dot(in_group, x, ((0,), (0,)), HIGH)
        keep = iota((width, MODES), 0) % MODES == iota((width, MODES), 1)
        ones = jnp.ones((MODES, width), f32)
        return dot(jnp.where(keep, wide, 0.0), ones, precision=HIGH)

    rate_col, scaled_col = column(rate), column(scaled)
    wide_lane = iota((width, width), 1)
    wide_row = iota((width, width), 0)
    same_i = (wide_row // MODES) % 4 == wide_lane // L
    at = (wide_lane % L).astype(f32)
    rise_cols = jnp.where(same_i, jnp.exp(at * rate_col), 0.0)
    fall_cols = jnp.where(same_i, scaled_col * jnp.exp(-at * rate_col), 0.0)

    def product(a, b):
        a_hi, a_lo = split(a)
        b_hi, b_lo = split(b)
        return dot(a_hi, b_hi) + (dot(a_lo, b_hi) + dot(a_hi, b_lo))

    row_at = wide_row % L
    col_at = wide_lane % L
    causal = row_at >= col_at
    filt = jnp.where(causal, product(fall_rows * scaled_row, rise_cols), 0.0).astype(bf16)
    anti = jnp.where(row_at <= col_at, product(rise_rows, fall_cols), 0.0).astype(bf16)

    gram = jnp.zeros((width, width), f32)
    cross = jnp.zeros((16, width), f32)
    for j in range(chunks):
        rows = pl.ds(j * L, L)
        hi = sh_s[rows, :]
        lhs = jnp.concatenate([hi * m for m in mask_q], axis=0)
        gram = gram + dot(lhs, spread_i(x_s[rows, :]), ((1,), (1,)))
        cross = cross + fwd_s[j] * bend_s[j]
    gram = jnp.where(causal, gram, 0.0)
    g_hi, g_lo = split(gram)
    r_hi = rise_cols.astype(bf16)
    within = dot(g_hi, r_hi, ((1,), (1,))) + dot(g_lo, r_hi, ((1,), (1,)))
    within = jnp.sum(within * fall_rows, axis=0, keepdims=True)
    same_group = ((wide_row // GROUP) == (wide_lane // GROUP)).astype(bf16)

    def group_row(z):
        hi, rest = z.astype(bf16), z - z.astype(bf16).astype(f32)
        mid, low = split(rest)
        s = dot(jnp.concatenate([hi, mid, low], axis=0), same_group)
        s = s[:16] + s[16:32] + s[32:]
        return jnp.sum(s * in_mode, axis=0, keepdims=True)

    wbox[me] = within + group_row(cross * decay_one)
    for peer in ids:
        copy = pltpu.make_async_remote_copy(
            src_ref=wbox.at[me],
            dst_ref=wbox.at[me],
            send_sem=send_sem.at[2, peer],
            recv_sem=recv_sem.at[2, me],
            device_id={"seq": peer},
            device_id_type=MESH,
        )
        copy.start()
        sends.append(copy)

    def block_rows(x):
        hi, lo = split(x)
        masks = [in_group[g : g + 1, :].astype(bf16) for g in range(16)]
        return (
            jnp.concatenate([hi * m for m in masks], axis=0),
            jnp.concatenate([lo * m for m in masks], axis=0),
        )

    def outer(table, blocks):
        t_hi, t_lo = table
        b_hi, b_lo = blocks
        return dot(t_hi, b_hi) + (dot(t_lo, b_hi) + dot(t_hi, b_lo))

    head = fall * jnp.exp(-rate_row) * scaled_row
    tail = rise * jnp.exp(-float(L) * rate_row) * scaled_row
    head_t, tail_t = split(head), split(tail)
    for j in range(chunks):
        rows = pl.ds(j * L, L)
        inner = pick_rows(dot(filt, spread_i(x_s[rows, :])), L)
        conv_s[rows, :] = inner + outer(head_t, block_rows(fwd_s[j]))
        inner = pick_rows(
            dot(anti, spread_i(sh_s[rows, :])) + dot(anti, spread_i(sl_s[rows, :])), L
        )
        grad_s[rows, :] = inner + outer(tail_t, block_rows(bwd_s[j]))

    def arrived(batch, peer):
        return pltpu.make_async_remote_copy(
            src_ref=box.at[batch, peer],
            dst_ref=box.at[batch, peer],
            send_sem=send_sem.at[batch, peer],
            recv_sem=recv_sem.at[batch, peer],
            device_id={"seq": peer},
            device_id_type=MESH,
        )

    for peer in ids:
        arrived(0, peer).wait_recv()
    entry_f = jnp.zeros((16, width), f32)
    for i in range(n - 1):
        entry_f = jnp.where(i < me, entry_f * decay_len + box[0, i].astype(f32), entry_f)
    entry_b = jnp.zeros((16, width), f32)
    for i in reversed(range(1, n)):
        entry_b = jnp.where(i > me, entry_b * decay_len + box[0, i].astype(f32), entry_b)
    blocks_f, blocks_b = block_rows(entry_f), block_rows(entry_b)
    for j in range(chunks):
        rows = pl.ds(j * L, L)
        ahead = jnp.exp(-float(j * L) * rate_row)
        behind = jnp.exp(-float(length - L - j * L) * rate_row)
        conv = conv_s[rows, :] + outer(split(head * ahead), blocks_f)
        grad = grad_s[rows, :] + outer(split(tail * behind), blocks_b)
        mixed_ref[rows, :] = (q_s[rows, :].astype(f32) * conv).astype(bf16)
        qgrad_ref[rows, :] = (c_s[rows, :].astype(f32) * conv).astype(bf16)
        kgrad_ref[rows, :] = (grad * v_s[rows, :].astype(f32)).astype(bf16)
        vgrad_ref[rows, :] = (grad * k_s[rows, :].astype(f32)).astype(bf16)

    for peer in ids:
        arrived(1, peer).wait_recv()
    for peer in ids:
        pltpu.make_async_remote_copy(
            src_ref=wbox.at[peer],
            dst_ref=wbox.at[peer],
            send_sem=send_sem.at[2, peer],
            recv_sem=recv_sem.at[2, peer],
            device_id={"seq": peer},
            device_id_type=MESH,
        ).wait_recv()
    prefix = jnp.zeros((16, width), f32)
    cross = jnp.zeros((16, width), f32)
    total = wbox[0]
    for i in range(1, n):
        last = jnp.where(i - 1 < me, box[0, i - 1], box[1, i - 1])
        here = jnp.where(i < me, box[1, i], box[0, i])
        prefix = prefix * decay_len + last.astype(f32)
        cross = cross + prefix * here.astype(f32)
        total = total + wbox[i]
    total = (total + group_row(cross * decay_one)) * factor_row
    rgrad_ref[...] = dot(total * in_group, in_mode, ((1,), (1,)), HIGH)
    for copy in sends:
        copy.wait_send()


def writer(*refs):
    count = len(refs) // 2
    sources, targets, sem = refs[:count], refs[count : 2 * count], refs[-1]
    copies = [
        pltpu.make_async_copy(src, dst, sem.at[i])
        for i, (src, dst) in enumerate(zip(sources, targets))
    ]
    for copy in copies:
        copy.start()
    for copy in copies:
        copy.wait()


def peer_table():
    offsets = [(a, b) for a in range(2) for b in range(8) if (a, b) != (0, 0)]
    offsets.sort(key=lambda o: -(2 * o[0] + min(o[1], 8 - o[1])))

    def peers(me, i):
        a, b = offsets[i]
        return ((me // 8 + a) % 2) * 8 + (me % 8 + b) % 8

    return peers


def body(query_gate, key_gate, values_in, cotangent, decay_rate, residues):
    length, width = query_gate.shape
    n = lax.axis_size("seq")
    chunks = length // L
    big = (length, width)
    shapes = [pltpu.VMEM(big, bf16)] * 4 + [pltpu.VMEM(residues.shape, f32)]
    vmem = pl.BlockSpec(memory_space=pltpu.VMEM)
    hbm = pl.BlockSpec(memory_space=pltpu.HBM)

    def stay(x):
        return pltpu.with_memory_space_constraint(x, pltpu.HBM)

    results = pl.pallas_call(
        lambda *refs: kernel(peer_table(), *refs),
        out_shape=shapes,
        in_specs=[hbm] * 6,
        out_specs=[vmem] * 5,
        scratch_shapes=[pltpu.VMEM(residues.shape, f32)] * 2
        + [pltpu.VMEM(big, bf16)] * 7
        + [pltpu.VMEM(big, f32)] * 2
        + [pltpu.VMEM((chunks, MODES, width), f32)] * 3
        + [
            pltpu.VMEM((2, n, MODES, width), bf16),
            pltpu.VMEM((n, 1, width), f32),
            pltpu.SemaphoreType.DMA((6,)),
            pltpu.SemaphoreType.DMA((3, n)),
            pltpu.SemaphoreType.DMA((3, n)),
        ],
        compiler_params=pltpu.CompilerParams(
            collective_id=0, has_side_effects=True, vmem_limit_bytes=40 * 2**20
        ),
        name="scan",
    )(*map(stay, (query_gate, key_gate, values_in, cotangent, decay_rate, residues)))
    results = [pltpu.with_memory_space_constraint(r, pltpu.VMEM) for r in results]
    return tuple(
        pl.pallas_call(
            writer,
            out_shape=[jax.ShapeDtypeStruct(r.shape, r.dtype) for r in results],
            in_specs=[vmem] * 5,
            out_specs=[hbm] * 5,
            scratch_shapes=[pltpu.SemaphoreType.DMA((5,))],
            name="write",
        )(*results)
    )


def solution(mesh):
    wide = P("seq", "chan")
    small = P("chan", None)
    return jax.shard_map(
        body,
        mesh=mesh,
        in_specs=(wide,) * 4 + (small,) * 2,
        out_specs=(wide,) * 4 + (small,),
        check_vma=False,
    )
```

time: 180 us -> 22.8 us (0.13)
  the two profiles are of different devices: /device:TPU:128 before, /device:TPU:8 now
where the time goes in v1:
time: 22.8 us; the launch traced here: 22.7 us
  Pallas kernels  22 us (96%)
  between operations  0.64 us (3%)
    pallas_call x1, Pallas kernels, body(): pl.pallas_call(lambda *refs: kernel(peer_table(), *refs), out_shape=shape...  21 us
    pallas_call x1, Pallas kernels, body(): pl.pallas_call(writer, out_shape=[jax.ShapeDtypeStruct(r.shape, r.dtype)...  1.01 us

profile of v1, /device:TPU:8, one launch (start us, length us, event | category | flops | bytes accessed | tf_op | source)
XLA Modules:
  0.0 22.7 jit_solution(7572384849613611382)
XLA Ops:
  0.6 21.0 %scan.1 = (bf16[512,256]{1,0:T(8,128)(2,1)S(1)}, bf16[512,256]{1,0:T(8,128)(2,1)S(1)}, bf16[512,256]{1,0:T(8,128)(2,1)S(1)}, bf16[512,256]{1,0:T(8,128)(2,1)S(1)}, f32[16,16]{1,0:T(8,128)S(1)}) custom-call(bf16[512,256]{1,0:T(8,128)(2,1)} %refs_0_.1, bf16[512,256]{1,0:T(8,128)(2,1)} %refs_1_.1, bf16[512,256]{1,0:T(8,128)(2,1)} %refs_2_.1, ...), custom_call_target="tpu_custom_call" | custom-call | tf_op jit(solution)/shard_map/scan/pallas_call | solution.py:363
  21.6 1.0 %write.1 = (bf16[512,256]{1,0:T(8,128)(2,1)}, bf16[512,256]{1,0:T(8,128)(2,1)}, bf16[512,256]{1,0:T(8,128)(2,1)}, bf16[512,256]{1,0:T(8,128)(2,1)}, f32[16,16]{1,0:T(8,128)}) custom-call(bf16[512,256]{1,0:T(8,128)(2,1)S(1)} %get-tuple-element.10.refs_0_, bf16[512,256]{1,0:T(8,128)(2,1)S(1)} %get-tuple-element.11.refs_1_, ...), custom_call_target="tpu_custom_call" | custom-call | tf_op jit(solution)/shard_map/write/pallas_call | solution.py:386

commit v2 on v1

v2 whole, which is shorter than its diff:
```python
import jax
import jax.numpy as jnp
from jax import lax
from jax.experimental import pallas as pl
from jax.experimental.pallas import tpu as pltpu
from jax.sharding import PartitionSpec as P

MESH = pl.DeviceIdType.MESH
f32 = jnp.float32
bf16 = jnp.bfloat16
GROUP = 16
MODES = 16
L = 64
QUARTER = 64
HIGH = lax.Precision.HIGHEST


def dot(a, b, dims=((1,), (0,)), precision=None):
    return lax.dot_general(
        a, b, (dims, ((), ())), precision=precision, preferred_element_type=f32
    )


def split(x):
    hi = x.astype(bf16)
    return hi, (x - hi.astype(f32)).astype(bf16)


def iota(shape, axis):
    return lax.broadcasted_iota(jnp.int32, shape, axis)


def pick_rows(m, rows):
    left = iota((rows, 128), 1) < QUARTER
    return jnp.concatenate(
        [
            jnp.where(left, m[:rows, :128], m[rows : 2 * rows, :128]),
            jnp.where(left, m[2 * rows : 3 * rows, 128:], m[3 * rows :, 128:]),
        ],
        axis=1,
    )


def kernel(
    peers,
    q_hbm, k_hbm, v_hbm, c_hbm, rate_hbm, res_hbm,
    mixed_ref, qgrad_ref, kgrad_ref, vgrad_ref, rgrad_ref,
    small_s, kv_s, cq_s, x_s, sh_s, sl_s, conv_s, grad_s, fwd_s, bwd_s, bend_s,
    rise_s, fall_s, box, wbox, rbox, in_sem, send_sem, recv_sem, ready,
):
    length, width = x_s.shape
    chunks = length // L
    me = lax.axis_index("seq")
    n = lax.axis_size("seq")
    loads = (
        ((rate_hbm, small_s.at[0]), (res_hbm, small_s.at[1])),
        ((k_hbm, kv_s.at[0]), (v_hbm, kv_s.at[1])),
        ((c_hbm, cq_s.at[0]), (q_hbm, cq_s.at[1])),
    )
    for i, pair in enumerate(loads):
        for src, dst in pair:
            pltpu.make_async_copy(src, dst, in_sem.at[i]).start()

    def loaded(i):
        both = (small_s, kv_s, cq_s)[i]
        pltpu.make_async_copy(both, both, in_sem.at[i]).wait()

    k_s, v_s, c_s, q_s = kv_s.at[0], kv_s.at[1], cq_s.at[0], cq_s.at[1]
    ids = [peers(me, i) for i in range(n - 1)]
    column0 = lax.axis_index("chan") == 0
    first = me == 0
    collector = 1 + column0.astype(jnp.int32)
    middle = jnp.logical_and(me >= 4, me <= 6)
    late = jnp.logical_or(middle, me >= 10)
    late = jnp.logical_or(late, jnp.logical_and(column0, first))
    barrier = pltpu.get_barrier_semaphore()

    @pl.when(jnp.logical_not(jnp.logical_and(column0, first)))
    def _():
        for peer in ids:
            pl.semaphore_signal(
                barrier, inc=1, device_id={"seq": peer}, device_id_type=MESH
            )

    loaded(0)
    rate = small_s[0]
    factor = jnp.sqrt(1.0 - jnp.exp(-2.0 * rate))
    scaled = small_s[1] * factor
    lane_hi = iota((16, width), 1) // GROUP
    lane_lo = iota((16, width), 1) % GROUP
    row16 = iota((16, width), 0)
    in_group = (lane_hi == row16).astype(f32)
    in_mode = (lane_lo == row16).astype(f32)

    def thirds(x):
        hi, rest = x.astype(bf16), x - x.astype(bf16).astype(f32)
        mid, low = split(rest)
        return jnp.concatenate([hi, mid, low], axis=0)

    lane = iota((16, width), 1)
    picks = [row16 == quarter * 4 + lane // L for quarter in range(4)]
    picks = jnp.concatenate(picks + [lane_hi == row16], axis=1).astype(bf16)
    rates = dot(thirds(rate), jnp.concatenate([picks] * 3, axis=0), ((0,), (0,)))
    rate_mc = rates[:, 4 * width :]

    position = (lane % L).astype(f32)
    end_parts = []
    start_parts = []
    for quarter in range(4):
        here = rates[:, quarter * width : (quarter + 1) * width]
        end_parts.append(jnp.exp((position - (L - 1.0)) * here))
        start_parts.append(jnp.exp(-position * here))
    end_hi, end_lo = zip(*[split(x) for x in end_parts])
    start_hi, start_lo = zip(*[split(x) for x in start_parts])

    def halves(hi, lo):
        return [
            jnp.concatenate([hi[2 * h], hi[2 * h + 1], lo[2 * h], lo[2 * h + 1]], axis=0)
            for h in range(2)
        ]

    end_pow = halves(end_hi, end_lo)
    start_pow = halves(start_hi, start_lo)

    lane64 = iota((L, width), 1)
    mask_i = [((lane64 // GROUP) % 4 == i).astype(bf16) for i in range(4)]
    mask_q = [(lane64 // QUARTER == q).astype(bf16) for q in range(4)]

    def spread_i(x):
        return jnp.concatenate([x * m for m in mask_i], axis=0)

    left16 = iota((16, 128), 1) < QUARTER

    def state_of(tables, pieces):
        out = []
        for h in range(2):
            first, *rest = pieces
            r = dot(tables[h], first[:, 128 * h : 128 * h + 128])
            r = r[:32] + r[32:]
            for piece in rest:
                r = r + dot(tables[h][:32], piece[:, 128 * h : 128 * h + 128])
            out.append(jnp.where(left16, r[:16], r[16:]))
        return jnp.concatenate(out, axis=1)

    decay_chunk = jnp.exp(-float(L) * rate_mc)
    decay_len = jnp.exp(-float(length) * rate_mc)
    decay_one = jnp.exp(-rate_mc)

    loaded(1)
    state = jnp.zeros((16, width), f32)
    for j in range(chunks):
        rows = pl.ds(j * L, L)
        x = (k_s[rows, :].astype(f32) * v_s[rows, :].astype(f32)).astype(bf16)
        x_s[rows, :] = x
        fwd_s[j] = state
        state = state * decay_chunk + state_of(end_pow, [spread_i(x)])
    end_state = state.astype(bf16)

    loaded(2)
    state = jnp.zeros((16, width), f32)
    for j in reversed(range(chunks)):
        rows = pl.ds(j * L, L)
        hi, lo = split(c_s[rows, :].astype(f32) * q_s[rows, :].astype(f32))
        sh_s[rows, :] = hi
        sl_s[rows, :] = lo
        bwd_s[j] = state
        here = state_of(start_pow, [spread_i(hi), spread_i(lo)])
        bend_s[j] = here
        state = state * decay_chunk + here
    box[0, me] = state.astype(bf16)
    box[1, me] = end_state

    def row_of(x):
        return jnp.sum(dot(x, in_mode, precision=HIGH) * in_group, axis=0, keepdims=True)

    rate_row, scaled_row, factor_row = row_of(rate), row_of(scaled), row_of(factor)
    row_at, col_at = iota((width, width), 0) % L, iota((width, width), 1) % L
    causal = row_at >= col_at
    wide_lane = iota((width, width), 1)
    wide_row = iota((width, width), 0)
    same_group = ((wide_row // GROUP) == (wide_lane // GROUP)).astype(bf16)

    def group_row(z):
        hi, rest = z.astype(bf16), z - z.astype(bf16).astype(f32)
        mid, low = split(rest)
        s = dot(jnp.concatenate([hi, mid, low], axis=0), same_group)
        s = s[:16] + s[16:32] + s[32:]
        return jnp.sum(s * in_mode, axis=0, keepdims=True)


    step = iota((L, width), 0).astype(f32)
    fall = jnp.exp(-step * rate_row)
    rise = jnp.exp(step * rate_row)
    q_of = iota((L, width), 1) // QUARTER

    def by_quarter(x):
        return jnp.concatenate([jnp.where(q_of == q, x, 0.0) for q in range(4)], axis=0)

    def column(x):
        wide = dot(in_group, x, ((0,), (0,)), HIGH)
        keep = iota((width, MODES), 0) % MODES == iota((width, MODES), 1)
        ones = jnp.ones((MODES, width), f32)
        return dot(jnp.where(keep, wide, 0.0), ones, precision=HIGH)

    same_i = (wide_row // MODES) % 4 == wide_lane // L
    at = (wide_lane % L).astype(f32)

    def product(a, b):
        a_hi, a_lo = split(a)
        b_hi, b_lo = split(b)
        return dot(a_hi, b_hi) + (dot(a_lo, b_hi) + dot(a_hi, b_lo))

    def residue_part():
        rise_cols = jnp.where(same_i, jnp.exp(at * column(rate)), 0.0)
        fall_rows = by_quarter(fall)
        rise_s[...] = rise_cols
        fall_s[...] = fall_rows
        gram = jnp.zeros((width, width), f32)
        cross = jnp.zeros((16, width), f32)
        for j in range(chunks):
            rows = pl.ds(j * L, L)
            hi = sh_s[rows, :]
            lhs = jnp.concatenate([hi * m for m in mask_q], axis=0)
            gram = gram + dot(lhs, spread_i(x_s[rows, :]), ((1,), (1,)))
            cross = cross + fwd_s[j] * bend_s[j]
        gram = jnp.where(causal, gram, 0.0)
        g_hi, g_lo = split(gram)
        r_hi = rise_cols.astype(bf16)
        within = dot(g_hi, r_hi, ((1,), (1,))) + dot(g_lo, r_hi, ((1,), (1,)))
        within = jnp.sum(within * fall_rows, axis=0, keepdims=True)
        wbox[me] = within + group_row(cross * decay_one)

    def block_rows(x):
        hi, lo = split(x)
        masks = [in_group[g : g + 1, :].astype(bf16) for g in range(16)]
        return (
            jnp.concatenate([hi * m for m in masks], axis=0),
            jnp.concatenate([lo * m for m in masks], axis=0),
        )

    def outer(table, blocks):
        t_hi, t_lo = table
        b_hi, b_lo = blocks
        return dot(t_hi, b_hi) + (dot(t_lo, b_hi) + dot(t_hi, b_lo))

    head = fall * jnp.exp(-rate_row) * scaled_row
    tail = rise * jnp.exp(-float(L) * rate_row) * scaled_row
    head_t, tail_t = split(head), split(tail)

    def inner_part():
        rate_col, scaled_col = column(rate), column(scaled)
        fall_cols = jnp.where(same_i, scaled_col * jnp.exp(-at * rate_col), 0.0)
        filt = product(fall_s[...] * scaled_row, rise_s[...])
        anti = product(by_quarter(rise), fall_cols)
        filt = jnp.where(causal, filt, 0.0).astype(bf16)
        anti = jnp.where(row_at <= col_at, anti, 0.0).astype(bf16)
        for j in range(chunks):
            rows = pl.ds(j * L, L)
            inner = pick_rows(dot(filt, spread_i(x_s[rows, :])), L)
            conv_s[rows, :] = inner + outer(head_t, block_rows(fwd_s[j]))
            inner = pick_rows(
                dot(anti, spread_i(sh_s[rows, :])) + dot(anti, spread_i(sl_s[rows, :])), L
            )
            grad_s[rows, :] = inner + outer(tail_t, block_rows(bwd_s[j]))


    @pl.when(jnp.logical_not(late))
    def _():
        residue_part()
        inner_part()

    others_in = jnp.where(jnp.logical_and(column0, jnp.logical_not(first)), n - 2, n - 1)
    pl.semaphore_wait(barrier, others_in)

    def send(source, target, kind, peer):
        return pltpu.make_async_remote_copy(
            src_ref=source,
            dst_ref=target,
            send_sem=send_sem.at[kind],
            recv_sem=recv_sem.at[kind],
            device_id={"seq": peer},
            device_id_type=MESH,
        )

    def near(peer):
        later = (peer > me).astype(jnp.int32)
        return send(box.at[later, me], box.at[0, me], 0, peer)

    def far():
        other = (collector < me).astype(jnp.int32)
        return send(box.at[other, me], box.at[1, me], 1, collector)

    def partial_sum():
        return send(wbox.at[me], wbox.at[me], 2, collector)

    def result(peer):
        return send(rbox.at[0], rbox.at[0], 3, peer)

    def all_of(kind):
        some = pl.ds(0, n - 1)
        ref = (box.at[0, some], box.at[1, some], wbox.at[some], rbox.at[some])[kind]
        return send(ref, ref, kind, me)

    is_collector = me == collector

    @pl.when(jnp.logical_and(column0, first))
    def _():
        for peer in ids:
            pl.semaphore_signal(ready, inc=1, device_id={"seq": peer}, device_id_type=MESH)

    for place, peer in enumerate((0, 1, 8, 2, 7, 9, 15, 3, 6, 10, 14, 5, 11, 13, 4, 12)):
        wanted = me != peer
        if peer == 0:
            wanted = jnp.logical_and(wanted, jnp.logical_not(column0))

        @pl.when(wanted)
        def _():
            near(peer).start()

        if place == 3:

            @pl.when(jnp.logical_not(is_collector))
            def _():
                far().start()

    @pl.when(late)
    def _():
        residue_part()

    @pl.when(jnp.logical_not(is_collector))
    def _():
        partial_sum().start()

    @pl.when(late)
    def _():
        inner_part()

    @pl.when(jnp.logical_and(column0, jnp.logical_not(first)))
    def _():
        pl.semaphore_wait(ready, 1)
        near(0).start()

    all_of(0).wait_recv()
    entry_f = jnp.zeros((16, width), f32)
    for i in range(n - 1):
        entry_f = jnp.where(i < me, entry_f * decay_len + box[0, i].astype(f32), entry_f)
    entry_b = jnp.zeros((16, width), f32)
    for i in reversed(range(1, n)):
        entry_b = jnp.where(i > me, entry_b * decay_len + box[0, i].astype(f32), entry_b)

    @pl.when(is_collector)
    def _():
        all_of(1).wait_recv()
        all_of(2).wait_recv()
        prefix = jnp.zeros((16, width), f32)
        cross = jnp.zeros((16, width), f32)
        total = wbox[0]
        for i in range(1, n):
            last = jnp.where(i - 1 < me, box[0, i - 1], box[1, i - 1])
            here = jnp.where(i < me, box[1, i], box[0, i])
            prefix = prefix * decay_len + last.astype(f32)
            cross = cross + prefix * here.astype(f32)
            total = total + wbox[i]
        total = (total + group_row(cross * decay_one)) * factor_row
        rbox[0] = dot(total * in_group, in_mode, ((1,), (1,)), HIGH)
        for peer in ids:
            result(peer).start()

    blocks_f, blocks_b = block_rows(entry_f), block_rows(entry_b)
    for j in range(chunks):
        rows = pl.ds(j * L, L)
        ahead = jnp.exp(-float(j * L) * rate_row)
        behind = jnp.exp(-float(length - L - j * L) * rate_row)
        conv = conv_s[rows, :] + outer(split(head * ahead), blocks_f)
        grad = grad_s[rows, :] + outer(split(tail * behind), blocks_b)
        mixed_ref[rows, :] = (q_s[rows, :].astype(f32) * conv).astype(bf16)
        qgrad_ref[rows, :] = (c_s[rows, :].astype(f32) * conv).astype(bf16)
        kgrad_ref[rows, :] = (grad * v_s[rows, :].astype(f32)).astype(bf16)
        vgrad_ref[rows, :] = (grad * k_s[rows, :].astype(f32)).astype(bf16)


    @pl.when(jnp.logical_not(is_collector))
    def _():
        result(collector).wait_recv()

    rgrad_ref[...] = rbox[0]
    all_of(0).wait_send()

    @pl.when(is_collector)
    def _():
        all_of(3).wait_send()

    @pl.when(jnp.logical_not(is_collector))
    def _():
        far().wait_send()
        partial_sum().wait_send()


def writer(*refs):
    count = len(refs) // 2
    sources, targets, sem = refs[:count], refs[count : 2 * count], refs[-1]
    copies = [
        pltpu.make_async_copy(src, dst, sem.at[i])
        for i, (src, dst) in enumerate(zip(sources, targets))
    ]
    for copy in copies:
        copy.start()
    for copy in copies:
        copy.wait()


def peer_table():
    offsets = [(a, b) for a in range(2) for b in range(8) if (a, b) != (0, 0)]
    offsets.sort(key=lambda o: -(2 * o[0] + min(o[1], 8 - o[1])))

    def peers(me, i):
        a, b = offsets[i]
        return ((me // 8 + a) % 2) * 8 + (me % 8 + b) % 8

    return peers


def body(query_gate, key_gate, values_in, cotangent, decay_rate, residues):
    length, width = query_gate.shape
    n = lax.axis_size("seq")
    chunks = length // L
    big = (length, width)
    shapes = [pltpu.VMEM(big, bf16)] * 4 + [pltpu.VMEM(residues.shape, f32)]
    vmem = pl.BlockSpec(memory_space=pltpu.VMEM)
    hbm = pl.BlockSpec(memory_space=pltpu.HBM)

    def stay(x):
        return pltpu.with_memory_space_constraint(x, pltpu.HBM)

    results = pl.pallas_call(
        lambda *refs: kernel(peer_table(), *refs),
        out_shape=shapes,
        in_specs=[hbm] * 6,
        out_specs=[vmem] * 5,
        scratch_shapes=[pltpu.VMEM((2,) + residues.shape, f32)]
        + [pltpu.VMEM((2,) + big, bf16)] * 2
        + [pltpu.VMEM(big, bf16)] * 3
        + [pltpu.VMEM(big, f32)] * 2
        + [pltpu.VMEM((chunks, MODES, width), f32)] * 3
        + [
            pltpu.VMEM((width, width), f32),
            pltpu.VMEM((width, width), f32),
            pltpu.VMEM((2, n, MODES, width), bf16),
            pltpu.VMEM((n, 1, width), f32),
            pltpu.VMEM((n,) + residues.shape, f32),
            pltpu.SemaphoreType.DMA((3,)),
            pltpu.SemaphoreType.DMA((4,)),
            pltpu.SemaphoreType.DMA((4,)),
            pltpu.SemaphoreType.REGULAR,
        ],
        compiler_params=pltpu.CompilerParams(
            collective_id=0, has_side_effects=True, vmem_limit_bytes=40 * 2**20
        ),
        name="scan",
    )(*map(stay, (query_gate, key_gate, values_in, cotangent, decay_rate, residues)))
    results = [pltpu.with_memory_space_constraint(r, pltpu.VMEM) for r in results]
    return tuple(
        pl.pallas_call(
            writer,
            out_shape=[jax.ShapeDtypeStruct(r.shape, r.dtype) for r in results],
            in_specs=[vmem] * 5,
            out_specs=[hbm] * 5,
            scratch_shapes=[pltpu.SemaphoreType.DMA((5,))],
            name="write",
        )(*results)
    )


def solution(mesh):
    wide = P("seq", "chan")
    small = P("chan", None)
    return jax.shard_map(
        body,
        mesh=mesh,
        in_specs=(wide,) * 4 + (small,) * 2,
        out_specs=(wide,) * 4 + (small,),
        check_vma=False,
    )
```

time: 22.8 us -> 20.1 us (0.88)
  the two profiles are of different devices: /device:TPU:8 before, /device:TPU:4 now
where the time goes in v2:
time: 20.1 us; the launch traced here: 19.9 us
  Pallas kernels  19.3 us (96%)
  between operations  0.64 us (3%)
    pallas_call x1, Pallas kernels, body(): pl.pallas_call(lambda *refs: kernel(peer_table(), *refs), out_shape=shape...  18.3 us
    pallas_call x1, Pallas kernels, body(): pl.pallas_call(writer, out_shape=[jax.ShapeDtypeStruct(r.shape, r.dtype)...  1.01 us

profile of v2, /device:TPU:4, one launch (start us, length us, event | category | flops | bytes accessed | tf_op | source)
XLA Modules:
  0.0 19.9 jit_solution(17188998693656552814)
XLA Ops:
  0.6 18.3 %scan.1 = (bf16[512,256]{1,0:T(8,128)(2,1)S(1)}, bf16[512,256]{1,0:T(8,128)(2,1)S(1)}, bf16[512,256]{1,0:T(8,128)(2,1)S(1)}, bf16[512,256]{1,0:T(8,128)(2,1)S(1)}, f32[16,16]{1,0:T(8,128)S(1)}) custom-call(bf16[512,256]{1,0:T(8,128)(2,1)} %refs_0_.1, bf16[512,256]{1,0:T(8,128)(2,1)} %refs_1_.1, bf16[512,256]{1,0:T(8,128)(2,1)} %refs_2_.1, ...), custom_call_target="tpu_custom_call" | custom-call | tf_op jit(solution)/shard_map/scan/pallas_call | solution.py:435
  18.9 1.0 %write.1 = (bf16[512,256]{1,0:T(8,128)(2,1)}, bf16[512,256]{1,0:T(8,128)(2,1)}, bf16[512,256]{1,0:T(8,128)(2,1)}, bf16[512,256]{1,0:T(8,128)(2,1)}, f32[16,16]{1,0:T(8,128)}) custom-call(bf16[512,256]{1,0:T(8,128)(2,1)S(1)} %get-tuple-element.10.refs_0_, bf16[512,256]{1,0:T(8,128)(2,1)S(1)} %get-tuple-element.11.refs_1_, ...), custom_call_target="tpu_custom_call" | custom-call | tf_op jit(solution)/shard_map/write/pallas_call | solution.py:463

commit v3 on v2

--- a/solution.py
+++ b/solution.py
@@ -44,9 +44,9 @@
 def kernel(
     peers,
     q_hbm, k_hbm, v_hbm, c_hbm, rate_hbm, res_hbm,
-    mixed_ref, qgrad_ref, kgrad_ref, vgrad_ref, rgrad_ref,
+    mixed_ref, qgrad_ref, kgrad_ref, vgrad_ref, rrow_ref,
     small_s, kv_s, cq_s, x_s, sh_s, sl_s, conv_s, grad_s, fwd_s, bwd_s, bend_s,
-    rise_s, fall_s, box, wbox, rbox, in_sem, send_sem, recv_sem, ready,
+    rise_s, fall_s, head_s, tail_s, box, wbox, rbox, in_sem, send_sem, recv_sem, ready,
 ):
     length, width = x_s.shape
     chunks = length // L
@@ -69,10 +69,15 @@
     ids = [peers(me, i) for i in range(n - 1)]
     column0 = lax.axis_index("chan") == 0
     first = me == 0
-    collector = 1 + column0.astype(jnp.int32)
-    middle = jnp.logical_and(me >= 4, me <= 6)
-    late = jnp.logical_or(middle, me >= 10)
+    per = n // 2
+    place = lax.rem(me, per)
+    collectors = [column0.astype(jnp.int32), per]
+    own_half = me - place
+    is_collector = jnp.logical_or(me == collectors[0], me == collectors[1])
+    late = jnp.logical_and(me >= 3, me != 8)
     late = jnp.logical_or(late, jnp.logical_and(column0, first))
+    last = jnp.logical_and(me >= 12, me <= 14)
+    last = jnp.logical_or(last, jnp.logical_and(column0, first))
     barrier = pltpu.get_barrier_semaphore()
 
     @pl.when(jnp.logical_not(jnp.logical_and(column0, first)))
@@ -262,11 +267,18 @@
                 dot(anti, spread_i(sh_s[rows, :])) + dot(anti, spread_i(sl_s[rows, :])), L
             )
             grad_s[rows, :] = inner + outer(tail_t, block_rows(bwd_s[j]))
-
+            ahead = jnp.exp(-float(j * L) * rate_row)
+            behind = jnp.exp(-float(length - L - j * L) * rate_row)
+            head_s[0, rows, :], head_s[1, rows, :] = split(head * ahead)
+            tail_s[0, rows, :], tail_s[1, rows, :] = split(tail * behind)
+
+
+    @pl.when(jnp.logical_not(last))
+    def _():
+        residue_part()
 
     @pl.when(jnp.logical_not(late))
     def _():
-        residue_part()
         inner_part()
 
     others_in = jnp.where(jnp.logical_and(column0, jnp.logical_not(first)), n - 2, n - 1)
@@ -286,50 +298,57 @@
         later = (peer > me).astype(jnp.int32)
         return send(box.at[later, me], box.at[0, me], 0, peer)
 
-    def far():
-        other = (collector < me).astype(jnp.int32)
-        return send(box.at[other, me], box.at[1, me], 1, collector)
-
-    def partial_sum():
-        return send(wbox.at[me], wbox.at[me], 2, collector)
+    def far(peer):
+        other = (peer < me).astype(jnp.int32)
+        return send(box.at[other, me], box.at[1, me], 1, peer)
+
+    def partial_sum(peer):
+        return send(wbox.at[me], wbox.at[me], 2, peer)
 
     def result(peer):
         return send(rbox.at[0], rbox.at[0], 3, peer)
 
-    def all_of(kind):
-        some = pl.ds(0, n - 1)
+    def all_of(kind, count):
+        some = pl.ds(0, count)
         ref = (box.at[0, some], box.at[1, some], wbox.at[some], rbox.at[some])[kind]
         return send(ref, ref, kind, me)
 
-    is_collector = me == collector
+    def to_collectors(fn):
+        for peer in collectors:
+
+            @pl.when(me != peer)
+            def _():
+                fn(peer).start()
 
     @pl.when(jnp.logical_and(column0, first))
     def _():
         for peer in ids:
             pl.semaphore_signal(ready, inc=1, device_id={"seq": peer}, device_id_type=MESH)
 
-    for place, peer in enumerate((0, 1, 8, 2, 7, 9, 15, 3, 6, 10, 14, 5, 11, 13, 4, 12)):
-        wanted = me != peer
-        if peer == 0:
-            wanted = jnp.logical_and(wanted, jnp.logical_not(column0))
-
-        @pl.when(wanted)
-        def _():
-            near(peer).start()
-
-        if place == 3:
-
-            @pl.when(jnp.logical_not(is_collector))
+    @pl.when(jnp.logical_not(last))
+    def _():
+        to_collectors(partial_sum)
+
+    def send_near(peers):
+        for peer in peers:
+            wanted = me != peer
+            if peer == 0:
+                wanted = jnp.logical_and(wanted, jnp.logical_not(column0))
+
+            @pl.when(wanted)
             def _():
-                far().start()
-
-    @pl.when(late)
+                near(peer).start()
+
+    send_near((0, 1, 8, 2))
+    to_collectors(far)
+    send_near((7, 9, 15))
+
+    @pl.when(last)
     def _():
         residue_part()
-
-    @pl.when(jnp.logical_not(is_collector))
-    def _():
-        partial_sum().start()
+        to_collectors(partial_sum)
+
+    send_near((3, 6, 10, 14, 5, 11, 13, 4, 12))
 
     @pl.when(late)
     def _():
@@ -340,7 +359,28 @@
         pl.semaphore_wait(ready, 1)
         near(0).start()
 
-    all_of(0).wait_recv()
+    all_of(0, n - 1).wait_recv()
+    @pl.when(is_collector)
+    def _():
+        all_of(1, n - 1).wait_recv()
+        prefix = jnp.zeros((16, width), f32)
+        cross = jnp.zeros((16, width), f32)
+        for i in range(1, n):
+            last = jnp.where(i - 1 < me, box[0, i - 1], box[1, i - 1])
+            here = jnp.where(i < me, box[1, i], box[0, i])
+            prefix = prefix * decay_len + last.astype(f32)
+            cross = cross + prefix * here.astype(f32)
+        total = group_row(cross * decay_one)
+        all_of(2, n - 1).wait_recv()
+        for i in range(n):
+            total = total + wbox[i]
+        rbox[0] = total * factor_row
+        for peer in (0, 1, 7, 2, 6, 3, 5, 4):
+
+            @pl.when(place != peer)
+            def _():
+                result(own_half + peer).start()
+
     entry_f = jnp.zeros((16, width), f32)
     for i in range(n - 1):
         entry_f = jnp.where(i < me, entry_f * decay_len + box[0, i].astype(f32), entry_f)
@@ -348,63 +388,57 @@
     for i in reversed(range(1, n)):
         entry_b = jnp.where(i > me, entry_b * decay_len + box[0, i].astype(f32), entry_b)
 
-    @pl.when(is_collector)
-    def _():
-        all_of(1).wait_recv()
-        all_of(2).wait_recv()
-        prefix = jnp.zeros((16, width), f32)
-        cross = jnp.zeros((16, width), f32)
-        total = wbox[0]
-        for i in range(1, n):
-            last = jnp.where(i - 1 < me, box[0, i - 1], box[1, i - 1])
-            here = jnp.where(i < me, box[1, i], box[0, i])
-            prefix = prefix * decay_len + last.astype(f32)
-            cross = cross + prefix * here.astype(f32)
-            total = total + wbox[i]
-        total = (total + group_row(cross * decay_one)) * factor_row
-        rbox[0] = dot(total * in_group, in_mode, ((1,), (1,)), HIGH)
-        for peer in ids:
-            result(peer).start()
-
     blocks_f, blocks_b = block_rows(entry_f), block_rows(entry_b)
-    for j in range(chunks):
-        rows = pl.ds(j * L, L)
-        ahead = jnp.exp(-float(j * L) * rate_row)
-        behind = jnp.exp(-float(length - L - j * L) * rate_row)
-        conv = conv_s[rows, :] + outer(split(head * ahead), blocks_f)
-        grad = grad_s[rows, :] + outer(split(tail * behind), blocks_b)
+
+    def lifted(table, rows, blocks):
+        hi, lo = table[0, rows, :], table[1, rows, :]
+        return dot(hi, blocks[0]) + (dot(lo, blocks[0]) + dot(hi, blocks[1]))
+
+    for j in range(2):
+        rows = pl.ds(j * length // 2, length // 2)
+        conv = conv_s[rows, :] + lifted(head_s, rows, blocks_f)
         mixed_ref[rows, :] = (q_s[rows, :].astype(f32) * conv).astype(bf16)
         qgrad_ref[rows, :] = (c_s[rows, :].astype(f32) * conv).astype(bf16)
+        grad = grad_s[rows, :] + lifted(tail_s, rows, blocks_b)
         kgrad_ref[rows, :] = (grad * v_s[rows, :].astype(f32)).astype(bf16)
         vgrad_ref[rows, :] = (grad * k_s[rows, :].astype(f32)).astype(bf16)
 
-
     @pl.when(jnp.logical_not(is_collector))
     def _():
-        result(collector).wait_recv()
-
-    rgrad_ref[...] = rbox[0]
-    all_of(0).wait_send()
+        result(me).wait_recv()
+
+    rrow_ref[...] = rbox[0]
+    all_of(0, n - 1).wait_send()
 
     @pl.when(is_collector)
     def _():
-        all_of(3).wait_send()
+        all_of(3, per - 1).wait_send()
+        all_of(1, 1).wait_send()
+        all_of(2, 1).wait_send()
 
     @pl.when(jnp.logical_not(is_collector))
     def _():
-        far().wait_send()
-        partial_sum().wait_send()
+        all_of(1, 2).wait_send()
+        all_of(2, 2).wait_send()
 
 
 def writer(*refs):
-    count = len(refs) // 2
-    sources, targets, sem = refs[:count], refs[count : 2 * count], refs[-1]
+    *sources, row = refs[:5]
+    *targets, residue = refs[5:10]
+    small, sem = refs[10:]
     copies = [
         pltpu.make_async_copy(src, dst, sem.at[i])
         for i, (src, dst) in enumerate(zip(sources, targets))
     ]
     for copy in copies:
         copy.start()
+    shape = (GROUP, row.shape[1])
+    group, lane = iota(shape, 0), iota(shape, 1)
+    here = jnp.where(lane // MODES == group, row[...], 0.0)
+    mode = (lane % MODES == group).astype(f32)
+    small[...] = dot(here, mode, ((1,), (1,)), HIGH)
+    copies.append(pltpu.make_async_copy(small, residue, sem.at[4]))
+    copies[-1].start()
     for copy in copies:
         copy.wait()
 
@@ -425,7 +459,7 @@
     n = lax.axis_size("seq")
     chunks = length // L
     big = (length, width)
-    shapes = [pltpu.VMEM(big, bf16)] * 4 + [pltpu.VMEM(residues.shape, f32)]
+    shapes = [pltpu.VMEM(big, bf16)] * 4 + [pltpu.VMEM((1, width), f32)]
     vmem = pl.BlockSpec(memory_space=pltpu.VMEM)
     hbm = pl.BlockSpec(memory_space=pltpu.HBM)
 
@@ -445,9 +479,11 @@
         + [
             pltpu.VMEM((width, width), f32),
             pltpu.VMEM((width, width), f32),
+            pltpu.VMEM((2,) + big, bf16),
+            pltpu.VMEM((2,) + big, bf16),
             pltpu.VMEM((2, n, MODES, width), bf16),
             pltpu.VMEM((n, 1, width), f32),
-            pltpu.VMEM((n,) + residues.shape, f32),
+            pltpu.VMEM((n, 1, width), f32),
             pltpu.SemaphoreType.DMA((3,)),
             pltpu.SemaphoreType.DMA((4,)),
             pltpu.SemaphoreType.DMA((4,)),
@@ -462,10 +498,14 @@
     return tuple(
         pl.pallas_call(
             writer,
-            out_shape=[jax.ShapeDtypeStruct(r.shape, r.dtype) for r in results],
+            out_shape=[jax.ShapeDtypeStruct(big, bf16)] * 4
+            + [jax.ShapeDtypeStruct(residues.shape, f32)],
             in_specs=[vmem] * 5,
             out_specs=[hbm] * 5,
-            scratch_shapes=[pltpu.SemaphoreType.DMA((5,))],
+            scratch_shapes=[
+                pltpu.VMEM(residues.shape, f32),
+                pltpu.SemaphoreType.DMA((5,)),
+            ],
             name="write",
         )(*results)
     )

time: 20.1 us -> 18.3 us (0.910)
  the two profiles are of different devices: /device:TPU:4 before, /device:TPU:136 now
where the time goes in v3:
time: 18.3 us; the launch traced here: 18.2 us
  Pallas kernels  17.5 us (96%)
  between operations  0.64 us (3%)
    pallas_call x1, Pallas kernels, body(): pl.pallas_call(lambda *refs: kernel(peer_table(), *refs), out_shape=shape...  16.5 us
    pallas_call x1, Pallas kernels, body(): pl.pallas_call(writer, out_shape=[jax.ShapeDtypeStruct(big, bf16)] * 4 +...  1.01 us

profile of v3, /device:TPU:136, one launch (start us, length us, event | category | flops | bytes accessed | tf_op | source)
XLA Modules:
  0.0 18.2 jit_solution(13872374643940886884)
XLA Ops:
  0.6 16.5 %scan.1 = (bf16[512,256]{1,0:T(8,128)(2,1)S(1)}, bf16[512,256]{1,0:T(8,128)(2,1)S(1)}, bf16[512,256]{1,0:T(8,128)(2,1)S(1)}, bf16[512,256]{1,0:T(8,128)(2,1)S(1)}, f32[1,256]{1,0:T(1,128)S(1)}) custom-call(bf16[512,256]{1,0:T(8,128)(2,1)} %refs_0_.1, bf16[512,256]{1,0:T(8,128)(2,1)} %refs_1_.1, bf16[512,256]{1,0:T(8,128)(2,1)} %refs_2_.1, ...), custom_call_target="tpu_custom_call" | custom-call | tf_op jit(solution)/shard_map/scan/pallas_call | solution.py:469
  17.2 1.0 %write.1 = (bf16[512,256]{1,0:T(8,128)(2,1)}, bf16[512,256]{1,0:T(8,128)(2,1)}, bf16[512,256]{1,0:T(8,128)(2,1)}, bf16[512,256]{1,0:T(8,128)(2,1)}, f32[16,16]{1,0:T(8,128)}) custom-call(bf16[512,256]{1,0:T(8,128)(2,1)S(1)} %get-tuple-element.10.refs_0_, bf16[512,256]{1,0:T(8,128)(2,1)S(1)} %get-tuple-element.11.refs_1_, ...), custom_call_target="tpu_custom_call" | custom-call | tf_op jit(solution)/shard_map/write/pallas_call | solution.py:499

commit v4 on v3

--- a/solution.py
+++ b/solution.py
@@ -339,9 +339,8 @@
             def _():
                 near(peer).start()
 
-    send_near((0, 1, 8, 2))
     to_collectors(far)
-    send_near((7, 9, 15))
+    send_near((0, 1, 8, 2, 7, 9, 15))
 
     @pl.when(last)
     def _():

time: 18.3 us -> 18.2 us (level)
  the two profiles are of different devices: /device:TPU:136 before, /device:TPU:328 now
where the time goes in v4:
time: 18.2 us; the launch traced here: 18.1 us
  Pallas kernels  17.4 us (96%)
  between operations  0.64 us (4%)
    pallas_call x1, Pallas kernels, body(): pl.pallas_call(lambda *refs: kernel(peer_table(), *refs), out_shape=shape...  16.4 us
    pallas_call x1, Pallas kernels, body(): pl.pallas_call(writer, out_shape=[jax.ShapeDtypeStruct(big, bf16)] * 4 +...  1.01 us

profile of v4, /device:TPU:328, one launch (start us, length us, event | category | flops | bytes accessed | tf_op | source)
XLA Modules:
  0.0 18.1 jit_solution(1449343757137370069)
XLA Ops:
  0.6 16.4 %scan.1 = (bf16[512,256]{1,0:T(8,128)(2,1)S(1)}, bf16[512,256]{1,0:T(8,128)(2,1)S(1)}, bf16[512,256]{1,0:T(8,128)(2,1)S(1)}, bf16[512,256]{1,0:T(8,128)(2,1)S(1)}, f32[1,256]{1,0:T(1,128)S(1)}) custom-call(bf16[512,256]{1,0:T(8,128)(2,1)} %refs_0_.1, bf16[512,256]{1,0:T(8,128)(2,1)} %refs_1_.1, bf16[512,256]{1,0:T(8,128)(2,1)} %refs_2_.1, ...), custom_call_target="tpu_custom_call" | custom-call | tf_op jit(solution)/shard_map/scan/pallas_call | solution.py:468
  17.1 1.0 %write.1 = (bf16[512,256]{1,0:T(8,128)(2,1)}, bf16[512,256]{1,0:T(8,128)(2,1)}, bf16[512,256]{1,0:T(8,128)(2,1)}, bf16[512,256]{1,0:T(8,128)(2,1)}, f32[16,16]{1,0:T(8,128)}) custom-call(bf16[512,256]{1,0:T(8,128)(2,1)S(1)} %get-tuple-element.10.refs_0_, bf16[512,256]{1,0:T(8,128)(2,1)S(1)} %get-tuple-element.11.refs_1_, ...), custom_call_target="tpu_custom_call" | custom-call | tf_op jit(solution)/shard_map/write/pallas_call | solution.py:498
